TPU v7x, 512 devices: a whole 4x4x16 slice. The times are simulated.
512 devices in a mesh: sta: 128 (over z, y, core), sec: 4 (over x).
Axes of the slice: x: 4, y: 4, z: 16, core: 2. Of those that a mesh axis runs over, the one named last changes fastest.
Arguments:
- raw_traces: bfloat16 [49152, 4096], P('sta', 'sec'), may hold values from -1200 to 1200
- fir_taps: float32 [33], replicated, may hold values from -1 to 1
- tile_pairs: int32 [16384, 2], replicated, may hold values from 0 to 4095, as said below
- tile_count: int32 [16384], P('sta'), may hold values from 0 to 4
Outputs:
- coherency: float32 [16, 2, 12, 196608], P('sec', None, None, 'sta')
Inputs may be any that keep to these rules, and one draw needn't show every extreme that they name: `tile_pairs`: tile t belongs to owner t // 128 along sta. Device u along sta holds blocks u * 32 to (u + 1) * 32 - 1. Among the 256 block ids of one owner's tiles, exactly two are held by each device u, and those two are equal.
All inputs are finite; a program needn't handle non-finite values.
Results may differ from a plain program's by a relative error of at most 0.004.
Values may be sent and summed in bfloat16 or wider, within the bound.
A program may use at most 128 MiB of HBM per device.

v0:
```python
import functools
import math

import jax
import jax.numpy as jnp
import numpy as np
from jax import lax
from jax.experimental import pallas as pl
from jax.experimental.pallas import tpu as pltpu
from jax.sharding import PartitionSpec as P

MESH = pl.DeviceIdType.MESH
L = 4096
F = 1024
LOWBIN = 4
WB = 64
FH = 16
NH = 32
BR = 12
PLANE = 8
NZ = 16
NX = 4
REACH = 4
CROWS = 48
BLK = 4 * BR
F32 = jnp.float32
BF16 = jnp.bfloat16


def dft_tables():
    cols = np.arange(512)
    sect, part, band, mm = cols // 128, (cols // 64) % 2, (cols // 16) % 4, cols % 16
    m = (4 * sect + band) * 16 + mm + 1
    t = np.arange(1024)
    planes = []
    for r in (0, 2, 1, 3):
        angle = 2.0 * np.pi / L * ((t[:, None] * (4 * m + r)[None, :]) % L)
        planes.append(np.where(part[None, :] == 0, np.cos(angle), -np.sin(angle)))
    return np.concatenate(planes).astype(np.float32)


def split(value):
    high = value.astype(BF16)
    return high, (value - high.astype(F32)).astype(BF16)


def mm(a, b):
    return jnp.dot(a, b, preferred_element_type=F32)


def build_filters(taps_ref, toep_ref, box_ref):
    def rows(i, carry):
        start = pl.multiple_of(32 * i, 32)
        diff = (
            lax.broadcasted_iota(jnp.int32, (32, 256), 0)
            + 32 * i
            - lax.broadcasted_iota(jnp.int32, (32, 256), 1)
        )
        first = jnp.zeros((32, 256), F32)
        second = jnp.zeros((32, 256), F32)
        for k in range(2 * FH + 1):
            tap = taps_ref[k]
            first = jnp.where(diff == k + 112, tap, first)
            second = jnp.where(diff == k - 144, tap, second)
        for which, value in enumerate((first, second)):
            high, low = split(value)
            toep_ref[which, 0, pl.ds(start, 32)] = high
            toep_ref[which, 1, pl.ds(start, 32)] = low
        box_ref[0, pl.ds(start, 32)] = jnp.where(jnp.abs(diff - 128) <= NH, 1.0, 0.0).astype(BF16)
        box_ref[1, pl.ds(start, 32)] = jnp.where(jnp.abs(diff + 128) <= NH, 1.0, 0.0).astype(BF16)
        return carry

    lax.fori_loop(0, 8, rows, 0)


def split_tables(wide, tab_ref):
    def rows(i, carry):
        start = pl.multiple_of(32 * i, 32)
        for r in range(4):
            high, low = split(wide[pl.ds(1024 * r + start, 32)])
            tab_ref[0, r, pl.ds(start, 32)] = high
            tab_ref[1, r, pl.ds(start, 32)] = low
        return carry

    lax.fori_loop(0, 32, rows, 0)


def normalize(xin, toep_ref, box_ref, filt, mag):
    n = CROWS
    zero = jnp.zeros((n, 256), BF16)
    parts = [xin[q, :, 256 * k : 256 * k + 256] for q in range(4) for k in range(4)]
    x0 = jnp.concatenate([zero] + parts, axis=0)
    x1 = jnp.concatenate(parts + [zero], axis=0)
    filtered = (mm(x0, toep_ref[0, 0]) + mm(x1, toep_ref[1, 0])) + (
        mm(x0, toep_ref[0, 1]) + mm(x1, toep_ref[1, 1])
    )
    filt[...] = filtered.reshape(17, n, 256)
    high, low = split(jnp.abs(filtered))
    mag[0] = high.reshape(17, n, 256)
    mag[1] = low.reshape(17, n, 256)
    level = (
        mm(mag[0, 0:16].reshape(16 * n, 256), box_ref[0])
        + mm(mag[0, 1:17].reshape(16 * n, 256), box_ref[1])
    ) + (
        mm(mag[1, 0:16].reshape(16 * n, 256), box_ref[0])
        + mm(mag[1, 1:17].reshape(16 * n, 256), box_ref[1])
    )
    center = jnp.concatenate([filt[0:16, :, 128:256], filt[1:17, :, 0:128]], axis=-1)
    return center / (level.reshape(16, n, 256) * (1.0 / (2 * NH + 1)) + 1e-05)


def combine_quarters(normed):
    n = CROWS
    seg = normed.reshape(4, 4, n, 256)
    even, odd = seg[0] + seg[2], seg[1] + seg[3]
    flat = lambda v: jnp.concatenate([v[k] for k in range(4)], axis=-1)
    rows = [flat(even + odd), flat(even - odd)]
    rows += [jnp.concatenate([flat(seg[0] - seg[2]), flat(seg[1] - seg[3])], axis=0)]
    return [jnp.concatenate(split(value), axis=0) for value in rows]


def spectra_of(parts, tab_ref, half):
    n = CROWS
    cols = slice(256 * half, 256 * half + 256)

    def transform(both, r):
        rows = both.shape[0] // 2
        full = mm(both, tab_ref[0, r, :, cols])
        return full[:rows] + full[rows:] + mm(both[:rows], tab_ref[1, r, :, cols])

    s0, s2 = transform(parts[0], 0), transform(parts[1], 1)
    odd1, odd3 = transform(parts[2], 2), transform(parts[2], 3)
    lane = lax.broadcasted_iota(jnp.int32, (n, 256), 1)
    sign = jnp.where((lane // 64) % 2 == 0, 1.0, -1.0)

    def swap(value):
        return jnp.concatenate(
            [pltpu.roll(value[:, 128 * s : 128 * s + 128], 64, 1) for s in range(2)], axis=-1
        )

    s1 = odd1[:n] + sign * swap(odd1[n:])
    s3 = odd3[:n] - sign * swap(odd3[n:])
    return s0, s1, s2, s3


def whiten(spectra, stage, out_ref, half):
    n = CROWS
    power = sum(s * s for s in spectra)
    li = lax.broadcasted_iota(jnp.int32, (128, 128), 0)
    lj = lax.broadcasted_iota(jnp.int32, (128, 128), 1)
    group = jnp.where((li // 16) % 4 == (lj // 16) % 4, 1.0, 0.0).astype(BF16)
    tall = jnp.concatenate([power[:, 128 * s : 128 * s + 128] for s in range(2)], axis=0)
    high, low = split(tall)
    band = mm(high, group) + mm(low, group)
    scale = lax.rsqrt(band * (1.0 / WB) + 1e-06)
    slot = (lax.broadcasted_iota(jnp.int32, (n, 128), 1) // 16) % 4
    for s in range(2):
        sc = scale[n * s : n * s + n]
        parts = [spectra[r][:, 128 * s : 128 * s + 128] * sc for r in range(4)]
        for b in range(4):
            value = None
            for r in range(4):
                moved = parts[r] if r == b else pltpu.roll(parts[r], (16 * (r - b)) % 128, 1)
                value = moved if value is None else jnp.where(slot == r, moved, value)
            for k in range(4):
                stage[s, BLK * k + BR * b : BLK * k + BR * b + BR, :] = value[BR * k : BR * k + BR]
        out_ref[2 * half + s] = stage[s].astype(BF16).reshape(4, BLK, 128)


def column_masks(count_ref, mask_ref, valid_ref):
    row = (lax.broadcasted_iota(jnp.int32, (144, 128), 0) * 10923) >> 17
    lane = lax.broadcasted_iota(jnp.int32, (144, 128), 1)
    for cg in range(3):
        column = ((lane + 128 * cg) * 10923) >> 17
        mask_ref[cg] = jnp.where(row + 2 * (128 * cg // 24) == column, 1.0, 0.0)
    tile = lax.broadcasted_iota(jnp.int32, (128, 1536), 0)
    column = lax.broadcasted_iota(jnp.int32, (128, 1536), 1)
    offset = column - BR * tile
    spread = jnp.where((offset >= 0) & (offset < BR), 1.0, 0.0).astype(BF16)
    counts = jnp.broadcast_to(count_ref[...].astype(F32), (8, 128)).astype(BF16)
    column = lax.broadcasted_iota(jnp.int32, (8, 1536), 1)
    station = ((column - BR * ((column * 10923) >> 17)) * 10923) >> 15
    valid_ref[...] = jnp.where(station.astype(F32) < mm(counts, spread), 1.0 / WB, 0.0)


def gather_ends(got, ends, z, w, left, right, turned):
    sign = jnp.where(lax.broadcasted_iota(jnp.int32, (BLK, 128), 1) < 64, -1.0, 1.0)

    def place(end):
        step = ((end >> 8) - z) & (NZ - 1)
        order = jnp.where(step < NZ // 2, 2 * step, 2 * NZ - 1 - 2 * step)
        return ((end >> 5) & (PLANE - 1)) * NZ + order

    def four(g, carry):
        rows = pl.ds(pl.multiple_of(BLK * g, 16), BLK)
        for e in range(2):
            tiles = [got[place(ends[2 * w + e, 4 * g + k])].astype(F32) for k in range(4)]
            for b in range(4):
                value = jnp.concatenate([t[BR * b : BR * b + BR] for t in tiles], axis=0)
                if e == 0:
                    left[b, rows] = value.astype(BF16)
                else:
                    right[b, rows] = value.astype(BF16)
                    turned[b, rows] = (sign * pltpu.roll(value, 64, 1)).astype(BF16)
        return carry

    lax.fori_loop(0, 32, four, 0, unroll=8)


def tile_products(left, right, turned, mask_ref, valid_ref, out_ref):
    for b in range(4):
        for cg in range(12):
            first = 2 * (128 * cg // 24)
            rows = left[b, BR * first : BR * first + 144]
            cols = slice(128 * cg, 128 * cg + 128)
            other = jnp.concatenate([right[b, cols], turned[b, cols]], axis=0)
            full = lax.dot_general(
                rows, other, (((1,), (1,)), ((), ())), preferred_element_type=F32
            )
            total = jnp.zeros((24, 256), F32)
            for k in range(6):
                keep = mask_ref[cg % 3, 24 * k : 24 * k + 24]
                total += jnp.concatenate([keep, keep], axis=1) * full[24 * k : 24 * k + 24]
            short = total[:BR] + total[BR:]
            valid = valid_ref[0:1, cols]
            out_ref[b, :, 0, cols] = short[:, :128] * valid
            out_ref[b, :, 1, cols] = short[:, 128:] * valid


def whole_kernel(
    raw_ref, taps_hbm, ends_hbm, count_hbm, tab_hbm, out_ref,
    taps_ref, ends_ref, count_ref, wide, tab, xin, toep, box, filt, mag, stage, wsend, pick_v, pick_s, ends_s,
    near_stage, far_stage, got, left, right, turned, mask, valid,
    slot0, slot1, slot2, slot3, slot4, slot5, slot6, slot7, slot8,
    tab_sem, own_sem, xs_sem, xr_sem, bs_sem, br_sem, zs_sem, zr_sem,
    ps_sem, pr_sem, pk_sem,
):
    slots = (slot0, slot1, slot2, slot3, slot4, slot5, slot6, slot7, slot8)
    sta = lax.axis_index("sta")
    x = lax.axis_index("sec")
    z = sta // PLANE
    w = sta % PLANE

    def at(step, ww):
        return ((z + step + NZ) % NZ) * PLANE + ww

    def xpeer(i):
        return (x + i) % NX

    def from_x(i):
        return (x + NX - i) % NX

    barrier = pltpu.get_barrier_semaphore()

    def greet(peer):
        pl.semaphore_signal(barrier, inc=1, device_id=peer, device_id_type=MESH)

    for i in range(1, NX):
        greet((sta, xpeer(i)))
    greet((at(1, w), x))
    greet((at(-1, w), x))
    for i in range(1, PLANE):
        greet((at(0, (w + i) % PLANE), x))

    taps_copy = pltpu.make_async_copy(taps_hbm, taps_ref, pk_sem.at[2])
    taps_copy.start()
    all_ends_copy = pltpu.make_async_copy(ends_hbm, ends_ref, pk_sem.at[3])
    all_ends_copy.start()
    count_copy = pltpu.make_async_copy(count_hbm, count_ref, pk_sem.at[4])
    count_copy.start()
    tab_copy = pltpu.make_async_copy(tab_hbm, wide, tab_sem)
    ends_copy = pltpu.make_async_copy(
        ends_hbm.at[pl.ds(pl.multiple_of(16 * z, 16), 16)], ends_s, pk_sem.at[0]
    )
    ends_copy.start()

    def raw_rows(q, c):
        return raw_ref.at[pl.ds(pl.multiple_of(96 * q + CROWS * c, 16), CROWS)]

    def own_copy(c):
        return pltpu.make_async_copy(raw_rows(x, c), xin.at[c, x], own_sem.at[c])

    for c in range(2):
        own_copy(c).start()
    pl.semaphore_wait(barrier, NX - 1 + 2 + PLANE - 1)

    def raw_copy(c, i):
        return pltpu.make_async_remote_copy(
            src_ref=raw_rows(xpeer(i), c),
            dst_ref=xin.at[c, x],
            send_sem=xs_sem.at[c, i - 1],
            recv_sem=xr_sem.at[c, i - 1],
            device_id=(sta, xpeer(i)),
            device_id_type=MESH,
        )

    def raw_start(c):
        for i in (2, 1, 3):
            raw_copy(c, i).start()

    def raw_wait(c):
        own_copy(c).wait()
        for i in range(1, NX):
            dst = xin.at[c, from_x(i)]
            pltpu.make_async_copy(dst, dst, xr_sem.at[c, i - 1]).wait()

    raw_start(0)
    raw_start(1)
    tab_copy.start()

    taps_copy.wait()
    build_filters(taps_ref, toep, box)
    all_ends_copy.wait()
    lane = lax.broadcasted_iota(jnp.int32, (16, 128), 1)
    picks = jnp.zeros((16, 128), jnp.int32)

    def asked(step, source):
        rows = ends_ref[pl.ds(pl.multiple_of(16 * ((z + step + NZ) % NZ), 16), 16), :]
        return jnp.max(jnp.where(rows // 32 == source, rows % 32, 0), axis=1, keepdims=True)

    wanted = [(0, at(-s if s <= REACH else s - REACH, w)) for s in range(9)]
    wanted += [(h, at(-REACH, w)) for h in range(1, REACH + 1)]
    wanted += [(-h, at(REACH, w)) for h in range(1, REACH + 1)]
    for col, (step, source) in enumerate(wanted):
        picks = jnp.where(lane == col, asked(step, source), picks)
    pick_v[...] = picks
    pick_copy = pltpu.make_async_copy(pick_v, pick_s, pk_sem.at[1])
    pick_copy.start()
    count_copy.wait()
    column_masks(count_ref, mask, valid)
    tab_copy.wait()
    split_tables(wide, tab)
    pick_copy.wait()
    ends_copy.wait()

    def back_copy(c, s):
        i = (s - x + NX) % NX
        return pltpu.make_async_remote_copy(
            src_ref=wsend.at[c, s],
            dst_ref=slot0.at[pl.ds(8 * x + 4 * c, 4)],
            send_sem=bs_sem.at[c, i],
            recv_sem=br_sem.at[c, i],
            device_id=(sta, s),
            device_id_type=MESH,
        )

    def section_start(c, half):
        for s in (2 * half, 2 * half + 1):

            @pl.when(s != x)
            def _():
                back_copy(c, s).start()

    def back_wait(c, i):
        rows = slot0.at[pl.ds(8 * from_x(i) + 4 * c, 4)]
        pltpu.make_async_copy(rows, rows, br_sem.at[c, i]).wait()

    def ring_wait(d, h, c, i):
        rows = slots[h + 4 * d].at[pl.ds(8 * from_x(i) + 4 * c, 4)]
        pltpu.make_async_copy(rows, rows, zr_sem.at[d, h - 1, 4 * c + i]).wait()

    def ring_copy(d, h, c, i):
        rows = pl.ds(8 * from_x(i) + 4 * c, 4)
        return pltpu.make_async_remote_copy(
            src_ref=(slots[0] if h == 1 else slots[h - 1 + 4 * d]).at[rows],
            dst_ref=slots[h + 4 * d].at[rows],
            send_sem=zs_sem.at[d, h - 1, 4 * c + i],
            recv_sem=zr_sem.at[d, h - 1, 4 * c + i],
            device_id=(at(1 - 2 * d, w), x),
            device_id_type=MESH,
        )

    def ring_start(h, c, i):
        for d in range(2):
            if h > 1:
                ring_wait(d, h - 1, c, i)
            ring_copy(d, h, c, i).start()

    def first_start(c):
        for i in range(1, NX):
            back_wait(c, i)
            ring_start(1, c, i)

    def asked_block(ww, col):
        return jnp.clip(jnp.maximum(pick_s[2 * ww, col], pick_s[2 * ww + 1, col]), 0, 31)

    def place_copy(source, place, step, ww):
        return pltpu.make_async_remote_copy(
            src_ref=source,
            dst_ref=got.at[w * NZ + place],
            send_sem=ps_sem,
            recv_sem=pr_sem,
            device_id=(at(step, ww), x),
            device_id_type=MESH,
        )

    def near_picks(s):
        place = 0 if s == 0 else (2 * s - 1 if s <= REACH else 2 * (s - REACH))

        def one(i, carry):
            ww = (w + i) % PLANE
            near_stage[s, i] = slots[s][asked_block(ww, s)]
            place_copy(near_stage.at[s, i], place, 0, ww).start()
            return carry

        lax.fori_loop(1, PLANE, one, 0)
        got[w * NZ + place] = slots[s][asked_block(w, s)]

    def far_picks(d, k):
        col = 9 + 4 * d + k - 1
        place = 2 * (REACH + k) - 1 + (d if k < REACH else 0)
        block = slots[REACH + 4 * d]

        def one(i, carry):
            ww = i if k < REACH else 2 * i + d
            far_stage[d, k - 1, i] = block[asked_block(ww, col)]
            place_copy(far_stage.at[d, k - 1, i], place, k * (1 - 2 * d), ww).start()
            return carry

        lax.fori_loop(0, PLANE if k < REACH else PLANE // 2, one, 0)

    for c in range(2):
        raw_wait(c)
        parts = combine_quarters(normalize(xin.at[c], toep, box, filt, mag))
        whiten(spectra_of(parts, tab, 0), stage, wsend.at[c], 0)
        section_start(c, 0)
        if c == 1:
            first_start(0)
        whiten(spectra_of(parts, tab, 1), stage, wsend.at[c], 1)
        section_start(c, 1)
        slot0[pl.ds(8 * x + 4 * c, 4)] = wsend[c, x]
        ring_start(1, c, 0)
    for i in range(NX):
        ring_start(2, 0, i)
    first_start(1)
    for i in range(NX):
        ring_start(2, 1, i)
    near_picks(0)
    near_picks(1)
    near_picks(1 + REACH)
    for h in range(3, REACH + 1):
        for c in range(2):
            for i in range(NX):
                ring_start(h, c, i)
        near_picks(h - 1)
        near_picks(h - 1 + REACH)
    for c in range(2):
        for i in range(NX):
            for d in range(2):
                ring_wait(d, REACH, c, i)
    for k in range(REACH, 0, -1):
        for d in range(2):
            far_picks(d, k)
    near_picks(REACH)
    near_picks(2 * REACH)

    pltpu.make_async_copy(got.at[0:119], got.at[0:119], pr_sem).wait()
    gather_ends(got, ends_s, z, w, left, right, turned)
    tile_products(left, right, turned, mask, valid, out_ref)

    pltpu.make_async_copy(got.at[0:119], got.at[0:119], ps_sem).wait()
    for c in range(2):
        for i in range(1, NX):
            raw_copy(c, i).wait_send()
            back_copy(c, xpeer(i)).wait_send()
        for i in range(NX):
            for d in range(2):
                for h in range(1, REACH + 1):
                    ring_copy(d, h, c, i).wait_send()


def body(raw, taps, pairs, counts):
    ends = pairs.reshape(128, 128, 2).transpose(0, 2, 1).reshape(256, 128)
    any_spec = pl.BlockSpec(memory_space=pl.ANY)
    vmem = pl.BlockSpec(memory_space=pltpu.VMEM)
    dma = pltpu.SemaphoreType.DMA
    tiles = pltpu.VMEM((4, 1536, 128), BF16)
    result = pl.pallas_call(
        whole_kernel,
        out_shape=jax.ShapeDtypeStruct((4, BR, 2, 1536), F32),
        in_specs=[any_spec] * 5,
        out_specs=vmem,
        scratch_shapes=[
            pltpu.SMEM((33,), F32),
            pltpu.VMEM((256, 128), jnp.int32),
            pltpu.VMEM((1, 128), jnp.int32),
            pltpu.VMEM((4096, 512), F32),
            pltpu.VMEM((2, 4, 1024, 512), BF16),
            pltpu.VMEM((2, NX, CROWS, 1024), BF16),
            pltpu.VMEM((2, 2, 256, 256), BF16),
            pltpu.VMEM((2, 256, 256), BF16),
            pltpu.VMEM((17, CROWS, 256), F32),
            pltpu.VMEM((2, 17, CROWS, 256), BF16),
            pltpu.VMEM((4, 4 * BLK, 128), F32),
            pltpu.VMEM((2, 4, 4, BLK, 128), BF16),
            pltpu.VMEM((16, 128), jnp.int32),
            pltpu.SMEM((16, 128), jnp.int32),
            pltpu.SMEM((16, 128), jnp.int32),
            pltpu.VMEM((9, PLANE, BLK, 128), BF16),
            pltpu.VMEM((2, REACH, PLANE, BLK, 128), BF16),
            pltpu.VMEM((NZ * PLANE, BLK, 128), BF16),
            tiles, tiles, tiles,
            pltpu.VMEM((3, 144, 128), F32),
            pltpu.VMEM((8, 1536), F32),
        ]
        + [pltpu.VMEM((32, BLK, 128), BF16)] * 9
        + [
            dma, dma((2,)), dma((2, 3)), dma((2, 3)), dma((2, 4)), dma((2, 4)),
            dma((2, 4, 8)), dma((2, 4, 8)), dma, dma, dma((5,)),
        ],
        compiler_params=pltpu.CompilerParams(
            collective_id=0, has_side_effects=True, vmem_limit_bytes=60 << 20
        ),
        name="cross_spectra",
    )(raw, taps, ends, counts.reshape(1, 128), jnp.asarray(dft_tables()))
    return result.transpose(0, 2, 1, 3)


def solution(mesh):
    return jax.shard_map(
        body,
        mesh=mesh,
        in_specs=(P("sta", "sec"), P(), P(), P("sta")),
        out_specs=P("sec", None, None, "sta"),
        check_vma=False,
    )
```

profile of v0, /device:TPU:1, one launch (start us, length us, event | category | flops | bytes accessed | tf_op | source)
XLA Modules:
  0.0 87.8 jit_solution(8922233591714958570)
XLA Ops:
  0.0 85.9 %cross_spectra.1 = f32[4,12,2,1536]{3,2,1,0:T(2,128)} custom-call(bf16[384,1024]{1,0:T(8,128)(2,1)} %raw_ref.1, f32[33]{0:T(128)} %taps_hbm.1, s32[256,128]{1,0:T(8,128)} %bitcast.8, s32[1,128]{1,0:T(1,128)} %bitcast.9, f32[4096,512]{1,0:T(8,128)} %constant.2.clone.tab_hbm), custom_call_target="tpu_custom_call" | custom-call | tf_op jit(solution)/shard_map/cross_spectra/pallas_call | solution.py:478
  85.9 1.9 %copy.8 = f32[4,2,12,1536]{3,1,2,0:T(2,128)} copy(f32[4,2,12,1536]{3,1,2,0:T(2,128)} %bitcast.7) | data formatting | bytes 1179648
where the time goes:
time: 88.5 us; the launch traced here: 87.8 us
  Pallas kernels  85.9 us (97%)
  local copies, waits for them, and re-layouts  1.92 us (2%)
    pallas_call x1, Pallas kernels, body(): pl.pallas_call(whole_kernel, out_shape=jax.ShapeDtypeStruct((4, BR, 2, 15...  85.9 us
    unnamed x1, local copies, waits for them, and re-layouts  1.92 us

commit v1 on v0

--- a/solution.py
+++ b/solution.py
@@ -121,7 +121,7 @@
 
 def spectra_of(parts, tab_ref, half):
     n = CROWS
-    cols = slice(256 * half, 256 * half + 256)
+    cols = pl.ds(pl.multiple_of(256 * half, 256), 256)
 
     def transform(both, r):
         rows = both.shape[0] // 2
@@ -207,7 +207,7 @@
     lax.fori_loop(0, 32, four, 0, unroll=8)
 
 
-def tile_products(left, right, turned, mask_ref, valid_ref, out_ref):
+def tile_products(left, right, turned, mask_ref, valid_ref, made, out_ref, out_sem):
     for b in range(4):
         for cg in range(12):
             first = 2 * (128 * cg // 24)
@@ -223,17 +223,18 @@
                 total += jnp.concatenate([keep, keep], axis=1) * full[24 * k : 24 * k + 24]
             short = total[:BR] + total[BR:]
             valid = valid_ref[0:1, cols]
-            out_ref[b, :, 0, cols] = short[:, :128] * valid
-            out_ref[b, :, 1, cols] = short[:, 128:] * valid
+            made[b, :, 0, cols] = short[:, :128] * valid
+            made[b, :, 1, cols] = short[:, 128:] * valid
+        pltpu.make_async_copy(made.at[b], out_ref.at[b], out_sem.at[b]).start()
 
 
 def whole_kernel(
     raw_ref, taps_hbm, ends_hbm, count_hbm, tab_hbm, out_ref,
     taps_ref, ends_ref, count_ref, wide, tab, xin, toep, box, filt, mag, stage, wsend, pick_v, pick_s, ends_s,
-    near_stage, far_stage, got, left, right, turned, mask, valid,
+    near_stage, far_stage, got, left, right, turned, mask, valid, made,
     slot0, slot1, slot2, slot3, slot4, slot5, slot6, slot7, slot8,
     tab_sem, own_sem, xs_sem, xr_sem, bs_sem, br_sem, zs_sem, zr_sem,
-    ps_sem, pr_sem, pk_sem,
+    ps_sem, pr_sem, pk_sem, out_sem,
 ):
     slots = (slot0, slot1, slot2, slot3, slot4, slot5, slot6, slot7, slot8)
     sta = lax.axis_index("sta")
@@ -305,7 +306,6 @@
             pltpu.make_async_copy(dst, dst, xr_sem.at[c, i - 1]).wait()
 
     raw_start(0)
-    raw_start(1)
     tab_copy.start()
 
     taps_copy.wait()
@@ -328,6 +328,7 @@
     pick_copy.start()
     count_copy.wait()
     column_masks(count_ref, mask, valid)
+    raw_start(1)
     tab_copy.wait()
     split_tables(wide, tab)
     pick_copy.wait()
@@ -344,7 +345,22 @@
             device_id_type=MESH,
         )
 
+    def first_copy(d, s):
+        i = (s - x + NX) % NX
+        return pltpu.make_async_remote_copy(
+            src_ref=wsend.at[0, s],
+            dst_ref=slots[1 + 4 * d].at[pl.ds(8 * x, 4)],
+            send_sem=zs_sem.at[d, 0, i],
+            recv_sem=zr_sem.at[d, 0, i],
+            device_id=(at(1 - 2 * d, w), s),
+            device_id_type=MESH,
+        )
+
     def section_start(c, half):
+        if c == 0:
+            for s in (2 * half, 2 * half + 1):
+                for d in range(2):
+                    first_copy(d, s).start()
         for s in (2 * half, 2 * half + 1):
 
             @pl.when(s != x)
@@ -419,19 +435,21 @@
 
         lax.fori_loop(0, PLANE if k < REACH else PLANE // 2, one, 0)
 
+    mine = x // 2
     for c in range(2):
         raw_wait(c)
         parts = combine_quarters(normalize(xin.at[c], toep, box, filt, mag))
-        whiten(spectra_of(parts, tab, 0), stage, wsend.at[c], 0)
-        section_start(c, 0)
+        whiten(spectra_of(parts, tab, mine), stage, wsend.at[c], mine)
+        section_start(c, mine)
+        slot0[pl.ds(8 * x + 4 * c, 4)] = wsend[c, x]
         if c == 1:
-            first_start(0)
-        whiten(spectra_of(parts, tab, 1), stage, wsend.at[c], 1)
-        section_start(c, 1)
-        slot0[pl.ds(8 * x + 4 * c, 4)] = wsend[c, x]
-        ring_start(1, c, 0)
-    for i in range(NX):
-        ring_start(2, 0, i)
+            ring_start(1, 1, 0)
+            for i in range(NX):
+                ring_start(2, 0, i)
+        whiten(spectra_of(parts, tab, 1 - mine), stage, wsend.at[c], 1 - mine)
+        section_start(c, 1 - mine)
+    for i in range(1, NX):
+        back_wait(0, i)
     first_start(1)
     for i in range(NX):
         ring_start(2, 1, i)
@@ -456,8 +474,10 @@
 
     pltpu.make_async_copy(got.at[0:119], got.at[0:119], pr_sem).wait()
     gather_ends(got, ends_s, z, w, left, right, turned)
-    tile_products(left, right, turned, mask, valid, out_ref)
-
+    tile_products(left, right, turned, mask, valid, made, out_ref, out_sem)
+
+    for b in range(4):
+        pltpu.make_async_copy(made.at[b], out_ref.at[b], out_sem.at[b]).wait()
     pltpu.make_async_copy(got.at[0:119], got.at[0:119], ps_sem).wait()
     for c in range(2):
         for i in range(1, NX):
@@ -465,7 +485,9 @@
             back_copy(c, xpeer(i)).wait_send()
         for i in range(NX):
             for d in range(2):
-                for h in range(1, REACH + 1):
+                if c == 0:
+                    first_copy(d, xpeer(i)).wait_send()
+                for h in range(1 + (c == 0), REACH + 1):
                     ring_copy(d, h, c, i).wait_send()
 
 
@@ -479,7 +501,7 @@
         whole_kernel,
         out_shape=jax.ShapeDtypeStruct((4, BR, 2, 1536), F32),
         in_specs=[any_spec] * 5,
-        out_specs=vmem,
+        out_specs=any_spec,
         scratch_shapes=[
             pltpu.SMEM((33,), F32),
             pltpu.VMEM((256, 128), jnp.int32),
@@ -502,11 +524,12 @@
             tiles, tiles, tiles,
             pltpu.VMEM((3, 144, 128), F32),
             pltpu.VMEM((8, 1536), F32),
+            pltpu.VMEM((4, BR, 2, 1536), F32),
         ]
         + [pltpu.VMEM((32, BLK, 128), BF16)] * 9
         + [
             dma, dma((2,)), dma((2, 3)), dma((2, 3)), dma((2, 4)), dma((2, 4)),
-            dma((2, 4, 8)), dma((2, 4, 8)), dma, dma, dma((5,)),
+            dma((2, 4, 8)), dma((2, 4, 8)), dma, dma, dma((5,)), dma((4,)),
         ],
         compiler_params=pltpu.CompilerParams(
             collective_id=0, has_side_effects=True, vmem_limit_bytes=60 << 20

time: 88.5 us -> 86.9 us (0.982)
  Pallas kernels: 85.9 us -> 84.8 us
    pallas_call x1, Pallas kernels: 85.9 us -> 84.8 us  [body(): pl.pallas_call(whole_kernel, out_shape=jax.ShapeDtypeStruct((4, BR, 2, 15...]
where the time goes in v1:
time: 86.9 us; the launch traced here: 86.7 us
  Pallas kernels  84.8 us (98%)
  local copies, waits for them, and re-layouts  1.92 us (2%)
    pallas_call x1, Pallas kernels, body(): pl.pallas_call(whole_kernel, out_shape=jax.ShapeDtypeStruct((4, BR, 2, 15...  84.8 us
    unnamed x1, local copies, waits for them, and re-layouts  1.92 us

profile of v1, /device:TPU:1, one launch (start us, length us, event | category | flops | bytes accessed | tf_op | source)
XLA Modules:
  0.0 86.7 jit_solution(12116508683597857737)
XLA Ops:
  0.0 84.8 %cross_spectra.1 = f32[4,12,2,1536]{3,2,1,0:T(2,128)} custom-call(bf16[384,1024]{1,0:T(8,128)(2,1)} %raw_ref.1, f32[33]{0:T(128)} %taps_hbm.1, s32[256,128]{1,0:T(8,128)} %bitcast.8, s32[1,128]{1,0:T(1,128)} %bitcast.9, f32[4096,512]{1,0:T(8,128)} %constant.2.clone.tab_hbm), custom_call_target="tpu_custom_call" | custom-call | tf_op jit(solution)/shard_map/cross_spectra/pallas_call | solution.py:500
  84.8 1.9 %copy.8 = f32[4,2,12,1536]{3,1,2,0:T(2,128)} copy(f32[4,2,12,1536]{3,1,2,0:T(2,128)} %bitcast.7) | data formatting | bytes 1179648

commit v2 on v1

--- a/solution.py
+++ b/solution.py
@@ -422,15 +422,13 @@
         lax.fori_loop(1, PLANE, one, 0)
         got[w * NZ + place] = slots[s][asked_block(w, s)]
 
-    def far_picks(d, k):
-        col = 9 + 4 * d + k - 1
-        place = 2 * (REACH + k) - 1 + (d if k < REACH else 0)
-        block = slots[REACH + 4 * d]
-
+    def far_picks(k):
         def one(i, carry):
-            ww = i if k < REACH else 2 * i + d
-            far_stage[d, k - 1, i] = block[asked_block(ww, col)]
-            place_copy(far_stage.at[d, k - 1, i], place, k * (1 - 2 * d), ww).start()
+            for d in range(2):
+                ww = i if k < REACH else 2 * i + d
+                place = 2 * (REACH + k) - 1 + (d if k < REACH else 0)
+                far_stage[d, k - 1, i] = slots[REACH + 4 * d][asked_block(ww, 9 + 4 * d + k - 1)]
+                place_copy(far_stage.at[d, k - 1, i], place, k * (1 - 2 * d), ww).start()
             return carry
 
         lax.fori_loop(0, PLANE if k < REACH else PLANE // 2, one, 0)
@@ -466,9 +464,8 @@
         for i in range(NX):
             for d in range(2):
                 ring_wait(d, REACH, c, i)
-    for k in range(REACH, 0, -1):
-        for d in range(2):
-            far_picks(d, k)
+    for k in range(1, REACH + 1):
+        far_picks(k)
     near_picks(REACH)
     near_picks(2 * REACH)
 

time: 86.9 us -> 85.8 us (0.987)
  the two profiles are of different devices: /device:TPU:1 before, /device:TPU:32 now
where the time goes in v2:
time: 85.8 us; the launch traced here: 85.6 us
  Pallas kernels  83.7 us (98%)
  local copies, waits for them, and re-layouts  1.92 us (2%)
    pallas_call x1, Pallas kernels, body(): pl.pallas_call(whole_kernel, out_shape=jax.ShapeDtypeStruct((4, BR, 2, 15...  83.7 us
    unnamed x1, local copies, waits for them, and re-layouts  1.92 us

profile of v2, /device:TPU:32, one launch (start us, length us, event | category | flops | bytes accessed | tf_op | source)
XLA Modules:
  0.0 85.6 jit_solution(13138089735792926730)
XLA Ops:
  0.0 83.7 %cross_spectra.1 = f32[4,12,2,1536]{3,2,1,0:T(2,128)} custom-call(bf16[384,1024]{1,0:T(8,128)(2,1)} %raw_ref.1, f32[33]{0:T(128)} %taps_hbm.1, s32[256,128]{1,0:T(8,128)} %bitcast.8, s32[1,128]{1,0:T(1,128)} %bitcast.9, f32[4096,512]{1,0:T(8,128)} %constant.2.clone.tab_hbm), custom_call_target="tpu_custom_call" | custom-call | tf_op jit(solution)/shard_map/cross_spectra/pallas_call | solution.py:497
  83.7 1.9 %copy.8 = f32[4,2,12,1536]{3,1,2,0:T(2,128)} copy(f32[4,2,12,1536]{3,1,2,0:T(2,128)} %bitcast.7) | data formatting | bytes 1179648

commit v3 on v2

--- a/solution.py
+++ b/solution.py
@@ -204,7 +204,7 @@
                     turned[b, rows] = (sign * pltpu.roll(value, 64, 1)).astype(BF16)
         return carry
 
-    lax.fori_loop(0, 32, four, 0, unroll=8)
+    lax.fori_loop(0, 32, four, 0, unroll=16)
 
 
 def tile_products(left, right, turned, mask_ref, valid_ref, made, out_ref, out_sem):
@@ -297,7 +297,18 @@
 
     def raw_start(c):
         for i in (2, 1, 3):
-            raw_copy(c, i).start()
+            if c == 1:
+                raw_copy(c, i).start()
+                continue
+            for part in range(3):
+                pltpu.make_async_remote_copy(
+                    src_ref=raw_ref.at[pl.ds(pl.multiple_of(96 * xpeer(i) + 16 * part, 16), 16)],
+                    dst_ref=xin.at[0, x, 16 * part : 16 * part + 16],
+                    send_sem=xs_sem.at[0, i - 1],
+                    recv_sem=xr_sem.at[0, i - 1],
+                    device_id=(sta, xpeer(i)),
+                    device_id_type=MESH,
+                ).start()
 
     def raw_wait(c):
         own_copy(c).wait()
@@ -306,6 +317,7 @@
             pltpu.make_async_copy(dst, dst, xr_sem.at[c, i - 1]).wait()
 
     raw_start(0)
+    raw_start(1)
     tab_copy.start()
 
     taps_copy.wait()
@@ -328,7 +340,6 @@
     pick_copy.start()
     count_copy.wait()
     column_masks(count_ref, mask, valid)
-    raw_start(1)
     tab_copy.wait()
     split_tables(wide, tab)
     pick_copy.wait()

time: 85.8 us -> 85.5 us (level)
  no operation moved by 1% of the time
where the time goes in v3:
time: 85.5 us; the launch traced here: 85.3 us
  Pallas kernels  83.4 us (98%)
  local copies, waits for them, and re-layouts  1.92 us (2%)
    pallas_call x1, Pallas kernels, body(): pl.pallas_call(whole_kernel, out_shape=jax.ShapeDtypeStruct((4, BR, 2, 15...  83.4 us
    unnamed x1, local copies, waits for them, and re-layouts  1.92 us

profile of v3, /device:TPU:32, one launch (start us, length us, event | category | flops | bytes accessed | tf_op | source)
XLA Modules:
  0.0 85.3 jit_solution(3076631847934901101)
XLA Ops:
  0.0 83.4 %cross_spectra.1 = f32[4,12,2,1536]{3,2,1,0:T(2,128)} custom-call(bf16[384,1024]{1,0:T(8,128)(2,1)} %raw_ref.1, f32[33]{0:T(128)} %taps_hbm.1, s32[256,128]{1,0:T(8,128)} %bitcast.8, s32[1,128]{1,0:T(1,128)} %bitcast.9, f32[4096,512]{1,0:T(8,128)} %constant.2.clone.tab_hbm), custom_call_target="tpu_custom_call" | custom-call | tf_op jit(solution)/shard_map/cross_spectra/pallas_call | solution.py:508
  83.4 1.9 %copy.8 = f32[4,2,12,1536]{3,1,2,0:T(2,128)} copy(f32[4,2,12,1536]{3,1,2,0:T(2,128)} %bitcast.7) | data formatting | bytes 1179648
